TPU v7x, 32 devices: a whole 2x2x4 slice. The times are simulated.
32 devices in a mesh: grp: 2 (over y), row: 4 (over z), col: 4 (over x, core).
Axes of the slice: x: 2, y: 2, z: 4, core: 2. Of those that a mesh axis runs over, the one named last changes fastest.
Arguments:
- src_elem: bfloat16 [4, 4, 512, 512], P('row', 'grp', 'col'), parts along dimension 1, may hold values from -0.25 to 0.25
- snk_elem: bfloat16 [8, 4, 512, 512], P('col', 'grp', 'row'), parts along dimension 1, may hold values from -0.25 to 0.25
- peramb: bfloat16 [4, 8, 4, 512, 512], P('row', 'col', 'grp'), parts along dimension 2, may hold values from -0.15625 to 0.15625
- insertions: int32 [2, 16], replicated, may hold values from 0 to 15, each once within a row
Outputs:
- blocks: float32 [2, 32, 4, 8], P(None, 'grp', 'row', 'col'), parts along dimension 1
There are 2 independent parts, one for each index of `grp`. A program takes and returns all parts, laid end to end along the dimension named above; an argument that names none is the same for every part. Nothing has to cross between parts.
Inputs may be any that keep to these rules, and one draw needn't show every extreme that they name: Each of the two rows of insertions names every code once.
All inputs are finite; a program needn't handle non-finite values.
Results may differ from a plain program's by a relative error of at most 0.0003.
Values may be sent and summed in bfloat16 or wider, within the bound.
A program may use at most 64 MiB of HBM per device.

v0:
```python
import functools

import jax
import jax.numpy as jnp
import numpy as np
from jax import lax
from jax.experimental import pallas as pl
from jax.experimental.pallas import tpu as pltpu
from jax.sharding import PartitionSpec as P

MESH = pl.DeviceIdType.MESH
HIGH = lax.Precision.HIGHEST
SUB = 16


def gamma_tables():
    pauli = [
        np.array([[0, 1], [1, 0]], complex),
        np.array([[0, -1j], [1j, 0]], complex),
        np.array([[1, 0], [0, -1]], complex),
    ]
    basis = []
    for sigma in pauli:
        part = np.zeros((4, 4), complex)
        part[0:2, 2:4] = -1j * sigma
        part[2:4, 0:2] = 1j * sigma
        basis.append(part)
    fourth = np.zeros((4, 4), complex)
    fourth[0:2, 2:4] = np.eye(2)
    fourth[2:4, 0:2] = np.eye(2)
    basis.append(fourth)
    tables = []
    for subset in range(16):
        prod = np.eye(4, dtype=complex)
        for bit_index in range(4):
            if subset >> bit_index & 1:
                prod = prod @ basis[bit_index]
        tables.append(prod)
    return np.stack(tables)


def insertion_tables(sinks):
    gam = gamma_tables()
    parts = (gam.real, gam.imag)
    second = np.zeros((16, 2, 2, 4, 4, 4, 4, 2, 2), np.float32)
    first = np.zeros((16, 2, 2, 2, 4, 128), np.float32)
    for part in range(2):
        for c in range(2):
            for u in range(4):
                second[:, part, c, u, :, u, :, c, :] = parts[part].transpose(0, 2, 1)[..., None]
                for out in range(2):
                    for sink in range(sinks):
                        for s in range(4):
                            for d in range(2):
                                own = (part + c + d + out) % 2
                                sign = (-1.0) ** ((own + part + c + d - out) // 2)
                                first[:, out, part, c, u, sink * 8 + s * 2 + d] = sign * parts[own][:, s, u]
    return second.reshape(16, 4096), first.reshape(16, 4096)


def split(value):
    high = value.astype(jnp.bfloat16)
    low = (value - high.astype(jnp.float32)).astype(jnp.bfloat16)
    return high, low


def dot_trans(left, right):
    return lax.dot_general(left, right, (((1,), (1,)), ((), ())), preferred_element_type=jnp.float32)


def kernel(
    rows, cols, src_ref, snk_ref, per_ref, ins_ref, second_ref, first_ref, out_ref,
    src_all, snk_all, per, per_g, lhs, rhs, diag, second, first, sel_second, sel_first,
    local_sem, src_send, src_recv, snk_send, snk_recv,
):
    row, col = lax.axis_index("row"), lax.axis_index("col")
    sinks = per.shape[0]
    order = per.shape[-1]
    evecs = order // 4
    groups = evecs // SUB
    src_rows = src_all.shape[2]
    snk_rows = snk_all.shape[3]

    barrier = pltpu.get_barrier_semaphore()
    for step in range(1, cols):
        pl.semaphore_signal(
            barrier, inc=1, device_id={"col": lax.rem(col + step, cols)}, device_id_type=MESH
        )

    @pl.when(row > 0)
    def _():
        pl.semaphore_signal(barrier, inc=1, device_id={"row": row - 1}, device_id_type=MESH)

    @pl.when(row < rows - 1)
    def _():
        pl.semaphore_signal(barrier, inc=1, device_id={"row": row + 1}, device_id_type=MESH)

    locals_ = [
        pltpu.make_async_copy(per_ref.at[0], per, local_sem.at[0]),
        pltpu.make_async_copy(src_ref.at[0], src_all.at[col], local_sem.at[1]),
        pltpu.make_async_copy(snk_ref, snk_all.at[row], local_sem.at[2]),
        pltpu.make_async_copy(second_ref, second, local_sem.at[3]),
        pltpu.make_async_copy(first_ref, first, local_sem.at[4]),
    ]
    for copy in locals_:
        copy.start()

    neighbours = (row + rows - 1) // rows + (2 * rows - 2 - row) // rows
    pl.semaphore_wait(barrier, cols - 1 + neighbours)

    def hop(shard, sink, way, source):
        return pltpu.make_async_remote_copy(
            src_ref=source,
            dst_ref=snk_all.at[shard, sink],
            send_sem=snk_send.at[way, shard, sink],
            recv_sem=snk_recv.at[shard, sink],
            device_id={"row": row + 1 - 2 * way},
            device_id_type=MESH,
        )

    for sink in range(sinks):

        @pl.when(row < rows - 1)
        def _():
            hop(row, sink, 0, snk_ref.at[sink]).start()

        @pl.when(row > 0)
        def _():
            hop(row, sink, 1, snk_ref.at[sink]).start()

    def spread(step):
        return pltpu.make_async_remote_copy(
            src_ref=src_ref.at[0],
            dst_ref=src_all.at[col],
            send_sem=src_send.at[step],
            recv_sem=src_recv.at[col],
            device_id={"col": lax.rem(col + step, cols)},
            device_id_type=MESH,
        )

    for step in range(1, cols):
        spread(step).start()

    def arrive(step, sink):
        below, above = row - 1 - step, row + 1 + step

        @pl.when(below >= 0)
        def _():
            hop(below, sink, 0, snk_all.at[below, sink]).wait_recv()

            @pl.when(row < rows - 1)
            def _():
                hop(below, sink, 0, snk_all.at[below, sink]).start()

        @pl.when(above < rows)
        def _():
            hop(above, sink, 1, snk_all.at[above, sink]).wait_recv()

            @pl.when(row > 0)
            def _():
                hop(above, sink, 1, snk_all.at[above, sink]).start()

    for copy in locals_:
        copy.wait()

    lanes = lax.broadcasted_iota(jnp.int32, (1, order), 1)
    signs = jnp.where(lanes < 2 * evecs, 1.0, -1.0).astype(jnp.bfloat16)

    def sign_sink(sink, carry):
        for c in range(2):
            per_g[sink, c] = per[sink, c] * signs
        return carry

    lax.fori_loop(0, sinks, sign_sink, 0)

    codes = lax.broadcasted_iota(jnp.int32, (16, 16), 0)

    def chosen(which, table):
        onehot = jnp.where(codes == ins_ref[which : which + 1, :], 1.0, 0.0).astype(jnp.bfloat16)
        return lax.dot_general(
            onehot, table[...], (((0,), (0,)), ((), ())), preferred_element_type=jnp.float32
        )

    pick = chosen(1, second)
    for block in range(16):
        sel_second[block * 16 : (block + 1) * 16, :] = pick[:, block * 256 : (block + 1) * 256]
    sel_first[...] = chosen(0, first)

    def forward_sink(sink, carry):
        for shard in range(cols):
            u, first_group = divmod(shard * src_rows, evecs)
            first_group //= SUB
            pair = src_all[shard].reshape(2 * src_rows, order)
            with_re = jnp.dot(pair, per[sink, 0], preferred_element_type=jnp.float32)
            with_im = jnp.dot(pair, per[sink, 1], preferred_element_type=jnp.float32)
            both = (
                with_re[:src_rows] - with_im[src_rows:],
                with_im[:src_rows] + with_re[src_rows:],
            )
            for c in range(2):
                for h, piece in enumerate(split(both[c])):
                    for v in range(4):
                        for near in range(src_rows // SUB):
                            g = first_group + near
                            lhs[sink, u, v, c, h, :, g * evecs : (g + 1) * evecs] = piece[
                                near * SUB : (near + 1) * SUB, v * evecs : (v + 1) * evecs
                            ]
        return carry

    width = 16 * SUB
    same = lax.broadcasted_iota(jnp.int32, (SUB, width), 0) == lax.rem(
        lax.broadcasted_iota(jnp.int32, (SUB, width), 1), SUB
    )
    mask = jnp.where(same, 1.0, 0.0).astype(jnp.float32)

    def contract(sink, w, pair):
        with_re = dot_trans(per_g[sink, 0], pair)
        with_im = dot_trans(per_g[sink, 1], pair)
        both = (
            with_re[:, :evecs] + with_im[:, evecs:],
            with_re[:, evecs:] - with_im[:, :evecs],
        )
        for c in range(2):
            for h, piece in enumerate(split(both[c])):
                for s in range(4):
                    for g in range(groups):
                        start = s * evecs + g * SUB
                        rhs[s, c, h, :, g * evecs : (g + 1) * evecs] = piece[start : start + SUB]
        right = rhs[...].reshape(width, groups * evecs)
        for u in range(4):
            left = lhs[sink, u].reshape(width, groups * evecs)
            full = dot_trans(left, right).reshape(16, SUB, width)
            diag[sink, w, u * 16 : (u + 1) * 16, :] = jnp.sum(full * mask[None], axis=1)

    def whole_shard(shard, sink):
        contract(sink, shard, snk_all[shard, sink].reshape(2 * evecs, order))

    def both_ways(step, sink):
        def one(way, carry):
            shard = row + (2 * way - 1) * (1 + step)

            @pl.when(jnp.logical_and(shard >= 0, shard < rows))
            def _():
                whole_shard(shard, sink)

            return carry

        lax.fori_loop(0, 2, one, 0)

    def wait_sources():
        for step in range(1, cols):
            other = lax.rem(col + step, cols)
            pltpu.make_async_remote_copy(
                src_ref=src_ref.at[0],
                dst_ref=src_all.at[other],
                send_sem=src_send.at[step],
                recv_sem=src_recv.at[other],
                device_id={"col": other},
                device_id_type=MESH,
            ).wait_recv()

    if snk_rows == evecs:
        for sink in range(sinks):
            arrive(0, sink)
        wait_sources()
        lax.fori_loop(0, sinks, forward_sink, 0)

        def own(sink, carry):
            whole_shard(row, sink)
            return carry

        lax.fori_loop(0, sinks, own, 0)
        for step in range(1, rows - 1):
            for sink in range(sinks):
                arrive(step, sink)
                if step < rows - 2:
                    both_ways(step - 1, sink)
                else:
                    if sink == 0:
                        lax.fori_loop(
                            0, sinks, lambda k, carry: (both_ways(step - 1, k), carry)[1], 0
                        )
                    both_ways(step, sink)
    else:
        def pass_on(step, carry):
            for sink in range(sinks):
                arrive(step, sink)
            return carry

        lax.fori_loop(0, rows - 1, pass_on, 0)
        wait_sources()
        lax.fori_loop(0, sinks, forward_sink, 0)
        many = evecs // snk_rows

        def gathered(index, carry):
            sink, w = index // 4, lax.rem(index, 4)
            pieces = [snk_all[w * many + near, sink, c] for c in range(2) for near in range(many)]
            contract(sink, w, jnp.concatenate(pieces, axis=0))
            return carry

        lax.fori_loop(0, 4 * sinks, gathered, 0)

    at = lax.broadcasted_iota(jnp.int32, (width, 128), 0)
    to = lax.broadcasted_iota(jnp.int32, (width, 128), 1)
    fits = jnp.logical_and(at // 64 == lax.rem(to, 8) // 2, lax.rem(at // 32, 2) == lax.rem(to, 2))
    signed = jnp.where(fits, jnp.where(at < 128, 1.0, -1.0), 0.0).astype(jnp.float32)
    spins = jnp.zeros((256, 128), jnp.float32)
    for sink in range(sinks):
        place = jnp.where(to // 8 == sink, signed, 0.0)
        spins += jnp.dot(
            diag[sink].reshape(256, width), place, precision=HIGH, preferred_element_type=jnp.float32
        )
    mixed = jnp.dot(sel_second[...], spins, precision=HIGH, preferred_element_type=jnp.float32)
    lane = lax.broadcasted_iota(jnp.int32, (16, 128), 1)
    spot = lax.broadcasted_iota(jnp.int32, (16, sinks), 1)
    for out in range(2):
        total = jnp.zeros((16, 128), jnp.float32)
        for block in range(16):
            start = (out * 16 + block) * 128
            total += sel_first[:, start : start + 128] * mixed[block * 16 : (block + 1) * 16]
        result = jnp.zeros((16, sinks), jnp.float32)
        for sink in range(sinks):
            one = jnp.sum(jnp.where(lane // 8 == sink, total, 0.0), axis=1, keepdims=True)
            result = jnp.where(spot == sink, one, result)
        out_ref[out] = result

    for step in range(1, cols):
        spread(step).wait_send()

    def sent(shard, carry):
        for sink in range(sinks):

            @pl.when(jnp.logical_and(shard <= row, row < rows - 1))
            def _():
                hop(shard, sink, 0, snk_all.at[shard, sink]).wait_send()

            @pl.when(jnp.logical_and(shard >= row, row > 0))
            def _():
                hop(shard, sink, 1, snk_all.at[shard, sink]).wait_send()

        return carry

    lax.fori_loop(0, rows, sent, 0)


def shards(rows, cols, src_elem, snk_elem, peramb, insertions):
    sinks, order = peramb.shape[1], peramb.shape[-1]
    assert src_elem.shape[0] == 1 and sinks <= 16
    second, first = (jnp.asarray(table, jnp.bfloat16) for table in insertion_tables(sinks))
    anywhere = pl.BlockSpec(memory_space=pl.ANY)
    vmem = pl.BlockSpec(memory_space=pltpu.VMEM)
    half = jnp.bfloat16
    wide = order * 2
    blocks = pl.pallas_call(
        functools.partial(kernel, rows, cols),
        out_shape=jax.ShapeDtypeStruct((2, 16, sinks), jnp.float32),
        in_specs=[anywhere, anywhere, anywhere, vmem, anywhere, anywhere],
        out_specs=vmem,
        scratch_shapes=[
            pltpu.VMEM((cols,) + src_elem.shape[1:], half),
            pltpu.VMEM((rows,) + snk_elem.shape, half),
            pltpu.VMEM(peramb.shape[1:], half),
            pltpu.VMEM(peramb.shape[1:], half),
            pltpu.VMEM((sinks, 4, 4, 2, 2, SUB, wide), half),
            pltpu.VMEM((4, 2, 2, SUB, wide), half),
            pltpu.VMEM((sinks, 4, 64, 16 * SUB), jnp.float32),
            pltpu.VMEM((16, 4096), half),
            pltpu.VMEM((16, 4096), half),
            pltpu.VMEM((256, 256), jnp.float32),
            pltpu.VMEM((16, 4096), jnp.float32),
            pltpu.SemaphoreType.DMA((5,)),
            pltpu.SemaphoreType.DMA((cols,)),
            pltpu.SemaphoreType.DMA((cols,)),
            pltpu.SemaphoreType.DMA((2, rows, sinks)),
            pltpu.SemaphoreType.DMA((rows, sinks)),
        ],
        compiler_params=pltpu.CompilerParams(
            collective_id=0, has_side_effects=True, vmem_limit_bytes=40 * 1024 * 1024
        ),
    )(src_elem, snk_elem, peramb, insertions, second, first)
    return blocks[:, :, None, :]


def solution(mesh):
    placed = (
        P("row", "grp", "col", None),
        P("col", "grp", "row", None),
        P("row", "col", "grp", None, None),
        P(),
    )
    body = functools.partial(shards, mesh.shape["row"], mesh.shape["col"])
    return jax.shard_map(
        body, mesh=mesh, in_specs=placed, out_specs=P(None, "grp", "row", "col"), check_vma=False
    )
```

profile of v0, /device:TPU:0, one launch (start us, length us, event | category | flops | bytes accessed | tf_op | source)
XLA Modules:
  0.0 48.9 jit_solution(8208768000426866411)
XLA Ops:
  0.0 0.0 copy-start
  0.0 1.6 %copy-done = bf16[1,2,2,512,512]{4,3,2,1,0:T(8,128)(2,1)S(1)} copy-done((bf16[1,2,2,512,512]{4,3,2,1,0:T(8,128)(2,1)S(1)}, bf16[1,2,2,512,512]{4,3,2,1,0:T(8,128)(2,1)}, u32[]{:S(2)}) %copy-start) | copy-done | bytes 2097176
  1.6 0.0 copy-start.1
  1.6 1.0 %copy-done.1 = bf16[2,2,128,512]{3,2,1,0:T(8,128)(2,1)S(1)} copy-done((bf16[2,2,128,512]{3,2,1,0:T(8,128)(2,1)S(1)}, bf16[2,2,128,512]{3,2,1,0:T(8,128)(2,1)}, u32[]{:S(2)}) %copy-start.1) | copy-done | bytes 524312
  2.6 0.0 copy-start.2
  2.6 0.9 %copy-done.2 = bf16[1,2,128,512]{3,2,1,0:T(8,128)(2,1)S(1)} copy-done((bf16[1,2,128,512]{3,2,1,0:T(8,128)(2,1)S(1)}, bf16[1,2,128,512]{3,2,1,0:T(8,128)(2,1)}, u32[]{:S(2)}) %copy-start.2) | copy-done | bytes 262168
  3.6 0.0 copy-start.3
  3.6 0.9 %copy-done.3 = bf16[16,4096]{1,0:T(8,128)(2,1)S(1)} copy-done((bf16[16,4096]{1,0:T(8,128)(2,1)S(1)}, bf16[16,4096]{1,0:T(8,128)(2,1)}, u32[]{:S(2)}) %copy-start.3) | copy-done | bytes 131096
  4.5 0.0 copy-start.4
  4.5 0.9 %copy-done.4 = bf16[16,4096]{1,0:T(8,128)(2,1)S(1)} copy-done((bf16[16,4096]{1,0:T(8,128)(2,1)S(1)}, bf16[16,4096]{1,0:T(8,128)(2,1)}, u32[]{:S(2)}) %copy-start.4) | copy-done | bytes 131096
  5.4 0.0 copy-start.5
  5.4 0.7 %copy-done.5 = s32[2,16]{1,0:T(2,128)S(1)} copy-done((s32[2,16]{1,0:T(2,128)S(1)}, s32[2,16]{1,0:T(2,128)}, u32[]{:S(2)}) %copy-start.5) | copy-done | bytes 152
  6.1 42.2 %shard_map.64 = f32[2,16,2]{2,1,0:T(8,128)S(1)} custom-call(bf16[1,2,128,512]{3,2,1,0:T(8,128)(2,1)S(1)} %copy-done.2, bf16[2,2,128,512]{3,2,1,0:T(8,128)(2,1)S(1)} %copy-done.1, bf16[1,2,2,512,512]{4,3,2,1,0:T(8,128)(2,1)S(1)} %copy-done, s32[2,16]{1,0:T(2,128)S(1)} %copy-done.5, bf16[16,4096]{1,0:T(8,128)(2,1)S(1)} %copy-done.4, bf16[16,4096]{1,0:T(8,128)(2,1)S(1)} %copy-done.3), custom_call_target="tpu_custom_call" | custom-call | tf_op jit(solution)/shard_map/pallas_call | solution.py:354
  48.3 0.7 %copy.7 = f32[2,16,2]{1,2,0:T(2,128)} copy(f32[2,16,2]{2,1,0:T(8,128)S(1)} %shard_map.64) | data formatting | bytes 512 | tf_op jit(solution)/shard_map/pallas_call | solution.py:354
Async XLA Ops:
  0.0 1.6 %copy-start = (bf16[1,2,2,512,512]{4,3,2,1,0:T(8,128)(2,1)S(1)}, bf16[1,2,2,512,512]{4,3,2,1,0:T(8,128)(2,1)}, u32[]{:S(2)}) copy-start(bf16[1,2,2,512,512]{4,3,2,1,0:T(8,128)(2,1)} %per_ref.1) | copy-start | bytes 6291460
  1.6 1.0 %copy-start.1 = (bf16[2,2,128,512]{3,2,1,0:T(8,128)(2,1)S(1)}, bf16[2,2,128,512]{3,2,1,0:T(8,128)(2,1)}, u32[]{:S(2)}) copy-start(bf16[2,2,128,512]{3,2,1,0:T(8,128)(2,1)} %snk_ref.1) | copy-start | bytes 1572868
  2.6 0.9 %copy-start.2 = (bf16[1,2,128,512]{3,2,1,0:T(8,128)(2,1)S(1)}, bf16[1,2,128,512]{3,2,1,0:T(8,128)(2,1)}, u32[]{:S(2)}) copy-start(bf16[1,2,128,512]{3,2,1,0:T(8,128)(2,1)} %src_ref.1) | copy-start | bytes 786436
  3.6 0.9 %copy-start.3 = (bf16[16,4096]{1,0:T(8,128)(2,1)S(1)}, bf16[16,4096]{1,0:T(8,128)(2,1)}, u32[]{:S(2)}) copy-start(bf16[16,4096]{1,0:T(8,128)(2,1)} %constant.5.clone.first_ref) | copy-start | bytes 393220
  4.5 0.9 %copy-start.4 = (bf16[16,4096]{1,0:T(8,128)(2,1)S(1)}, bf16[16,4096]{1,0:T(8,128)(2,1)}, u32[]{:S(2)}) copy-start(bf16[16,4096]{1,0:T(8,128)(2,1)} %constant.4.clone.second_ref) | copy-start | bytes 393220
  5.4 0.7 %copy-start.5 = (s32[2,16]{1,0:T(2,128)S(1)}, s32[2,16]{1,0:T(2,128)}, u32[]{:S(2)}) copy-start(s32[2,16]{1,0:T(2,128)} %ins_ref.1) | copy-start | bytes 388
where the time goes:
time: 49.2 us; the launch traced here: 48.9 us
  Pallas kernels  42.2 us (86%)
  local copies, waits for them, and re-layouts  6.73 us (14%)
    pallas_call x1, Pallas kernels, shards(): pl.pallas_call(functools.partial(kernel, rows, cols), out_shape=jax.Shape...  42.2 us
    unnamed x12, local copies, waits for them, and re-layouts  6.07 us

commit v1 on v0

--- a/solution.py
+++ b/solution.py
@@ -9,7 +9,6 @@
 from jax.sharding import PartitionSpec as P
 
 MESH = pl.DeviceIdType.MESH
-HIGH = lax.Precision.HIGHEST
 SUB = 16
 
 
@@ -70,7 +69,7 @@
 
 def kernel(
     rows, cols, src_ref, snk_ref, per_ref, ins_ref, second_ref, first_ref, out_ref,
-    src_all, snk_all, per, per_g, lhs, rhs, diag, second, first, sel_second, sel_first,
+    src_all, snk_all, per, per_g, lhs, rhs, spins, ins, second, first, sel_second, sel_first,
     local_sem, src_send, src_recv, snk_send, snk_recv,
 ):
     row, col = lax.axis_index("row"), lax.axis_index("col")
@@ -101,6 +100,7 @@
         pltpu.make_async_copy(snk_ref, snk_all.at[row], local_sem.at[2]),
         pltpu.make_async_copy(second_ref, second, local_sem.at[3]),
         pltpu.make_async_copy(first_ref, first, local_sem.at[4]),
+        pltpu.make_async_copy(ins_ref, ins, local_sem.at[5]),
     ]
     for copy in locals_:
         copy.start()
@@ -176,14 +176,16 @@
     codes = lax.broadcasted_iota(jnp.int32, (16, 16), 0)
 
     def chosen(which, table):
-        onehot = jnp.where(codes == ins_ref[which : which + 1, :], 1.0, 0.0).astype(jnp.bfloat16)
+        onehot = jnp.where(codes == ins[which : which + 1, :], 1.0, 0.0).astype(jnp.bfloat16)
         return lax.dot_general(
-            onehot, table[...], (((0,), (0,)), ((), ())), preferred_element_type=jnp.float32
+            onehot, table[...].astype(jnp.bfloat16), (((0,), (0,)), ((), ())), preferred_element_type=jnp.float32
         )
 
     pick = chosen(1, second)
     for block in range(16):
-        sel_second[block * 16 : (block + 1) * 16, :] = pick[:, block * 256 : (block + 1) * 256]
+        sel_second[block * 16 : (block + 1) * 16, :] = pick[
+            :, block * 256 : (block + 1) * 256
+        ].astype(jnp.bfloat16)
     sel_first[...] = chosen(0, first)
 
     def forward_sink(sink, carry):
@@ -213,6 +215,12 @@
     )
     mask = jnp.where(same, 1.0, 0.0).astype(jnp.float32)
 
+    at = lax.broadcasted_iota(jnp.int32, (width, 128), 0)
+    to = lax.broadcasted_iota(jnp.int32, (width, 128), 1)
+    fits = jnp.logical_and(at // 64 == lax.rem(to, 8) // 2, lax.rem(at // 32, 2) == lax.rem(to, 2))
+    signed = jnp.where(fits, jnp.where(at < 128, 1.0, -1.0), 0.0).astype(jnp.float32)
+    spins[...] = jnp.zeros_like(spins)
+
     def contract(sink, w, pair):
         with_re = dot_trans(per_g[sink, 0], pair)
         with_im = dot_trans(per_g[sink, 1], pair)
@@ -227,10 +235,16 @@
                         start = s * evecs + g * SUB
                         rhs[s, c, h, :, g * evecs : (g + 1) * evecs] = piece[start : start + SUB]
         right = rhs[...].reshape(width, groups * evecs)
+        sums = []
         for u in range(4):
             left = lhs[sink, u].reshape(width, groups * evecs)
             full = dot_trans(left, right).reshape(16, SUB, width)
-            diag[sink, w, u * 16 : (u + 1) * 16, :] = jnp.sum(full * mask[None], axis=1)
+            sums.append(jnp.sum(full * mask[None], axis=1))
+        place = jnp.where(to // 8 == sink, signed, 0.0).astype(jnp.bfloat16)
+        pair = jnp.concatenate(split(jnp.concatenate(sums, axis=0)), axis=1)
+        spins[w] += jnp.dot(
+            pair, jnp.concatenate([place, place], axis=0), preferred_element_type=jnp.float32
+        )
 
     def whole_shard(shard, sink):
         contract(sink, shard, snk_all[shard, sink].reshape(2 * evecs, order))
@@ -300,29 +314,24 @@
 
         lax.fori_loop(0, 4 * sinks, gathered, 0)
 
-    at = lax.broadcasted_iota(jnp.int32, (width, 128), 0)
-    to = lax.broadcasted_iota(jnp.int32, (width, 128), 1)
-    fits = jnp.logical_and(at // 64 == lax.rem(to, 8) // 2, lax.rem(at // 32, 2) == lax.rem(to, 2))
-    signed = jnp.where(fits, jnp.where(at < 128, 1.0, -1.0), 0.0).astype(jnp.float32)
-    spins = jnp.zeros((256, 128), jnp.float32)
-    for sink in range(sinks):
-        place = jnp.where(to // 8 == sink, signed, 0.0)
-        spins += jnp.dot(
-            diag[sink].reshape(256, width), place, precision=HIGH, preferred_element_type=jnp.float32
-        )
-    mixed = jnp.dot(sel_second[...], spins, precision=HIGH, preferred_element_type=jnp.float32)
-    lane = lax.broadcasted_iota(jnp.int32, (16, 128), 1)
-    spot = lax.broadcasted_iota(jnp.int32, (16, sinks), 1)
+    halves = jnp.concatenate(split(spins[...].reshape(256, 128)), axis=1)
+    mixed = jnp.dot(sel_second[...], halves, preferred_element_type=jnp.float32)
+    mixed = mixed[:, :128] + mixed[:, 128:]
+    totals = []
     for out in range(2):
         total = jnp.zeros((16, 128), jnp.float32)
         for block in range(16):
             start = (out * 16 + block) * 128
             total += sel_first[:, start : start + 128] * mixed[block * 16 : (block + 1) * 16]
-        result = jnp.zeros((16, sinks), jnp.float32)
-        for sink in range(sinks):
-            one = jnp.sum(jnp.where(lane // 8 == sink, total, 0.0), axis=1, keepdims=True)
-            result = jnp.where(spot == sink, one, result)
-        out_ref[out] = result
+        totals.append(total)
+    sink_of = lax.broadcasted_iota(jnp.int32, (16, 128), 1) // 8
+    member = jnp.where(sink_of == lax.broadcasted_iota(jnp.int32, (16, 128), 0), 1.0, 0.0)
+    ends = dot_trans(
+        member.astype(jnp.bfloat16), jnp.concatenate(split(jnp.concatenate(totals, axis=0)), axis=0)
+    )
+    ends = ends[:, :32] + ends[:, 32:]
+    for out in range(2):
+        out_ref[out] = ends[:sinks, out * 16 : (out + 1) * 16]
 
     for step in range(1, cols):
         spread(step).wait_send()
@@ -346,15 +355,15 @@
 def shards(rows, cols, src_elem, snk_elem, peramb, insertions):
     sinks, order = peramb.shape[1], peramb.shape[-1]
     assert src_elem.shape[0] == 1 and sinks <= 16
-    second, first = (jnp.asarray(table, jnp.bfloat16) for table in insertion_tables(sinks))
-    anywhere = pl.BlockSpec(memory_space=pl.ANY)
+    second, first = (jnp.asarray(table, jnp.float32) for table in insertion_tables(sinks))
+    anywhere = pl.BlockSpec(memory_space=pltpu.HBM)
     vmem = pl.BlockSpec(memory_space=pltpu.VMEM)
     half = jnp.bfloat16
     wide = order * 2
     blocks = pl.pallas_call(
         functools.partial(kernel, rows, cols),
-        out_shape=jax.ShapeDtypeStruct((2, 16, sinks), jnp.float32),
-        in_specs=[anywhere, anywhere, anywhere, vmem, anywhere, anywhere],
+        out_shape=jax.ShapeDtypeStruct((2, sinks, 16), jnp.float32),
+        in_specs=[anywhere] * 6,
         out_specs=vmem,
         scratch_shapes=[
             pltpu.VMEM((cols,) + src_elem.shape[1:], half),
@@ -363,22 +372,23 @@
             pltpu.VMEM(peramb.shape[1:], half),
             pltpu.VMEM((sinks, 4, 4, 2, 2, SUB, wide), half),
             pltpu.VMEM((4, 2, 2, SUB, wide), half),
-            pltpu.VMEM((sinks, 4, 64, 16 * SUB), jnp.float32),
-            pltpu.VMEM((16, 4096), half),
-            pltpu.VMEM((16, 4096), half),
-            pltpu.VMEM((256, 256), jnp.float32),
+            pltpu.VMEM((4, 64, 128), jnp.float32),
+            pltpu.VMEM(insertions.shape, jnp.int32),
             pltpu.VMEM((16, 4096), jnp.float32),
-            pltpu.SemaphoreType.DMA((5,)),
+            pltpu.VMEM((16, 4096), jnp.float32),
+            pltpu.VMEM((256, 256), half),
+            pltpu.VMEM((16, 4096), jnp.float32),
+            pltpu.SemaphoreType.DMA((6,)),
             pltpu.SemaphoreType.DMA((cols,)),
             pltpu.SemaphoreType.DMA((cols,)),
             pltpu.SemaphoreType.DMA((2, rows, sinks)),
             pltpu.SemaphoreType.DMA((rows, sinks)),
         ],
         compiler_params=pltpu.CompilerParams(
-            collective_id=0, has_side_effects=True, vmem_limit_bytes=40 * 1024 * 1024
+            collective_id=0, has_side_effects=True, vmem_limit_bytes=64 * 1024 * 1024
         ),
     )(src_elem, snk_elem, peramb, insertions, second, first)
-    return blocks[:, :, None, :]
+    return blocks.transpose(0, 2, 1)[:, :, None, :]
 
 
 def solution(mesh):

time: 49.2 us -> 43.6 us (0.89)
  local copies, waits for them, and re-layouts: 6.73 us -> 1.26 us
    unnamed x12 -> x1, local copies, waits for them, and re-layouts: 6.07 us -> 1.26 us
    pallas_call x1 -> x0, local copies, waits for them, and re-layouts: 0.66 us -> none  [shards(): pl.pallas_call(functools.partial(kernel, rows, cols), out_shape=jax.Shape...]
where the time goes in v1:
time: 43.6 us; the launch traced here: 43.5 us
  Pallas kernels  42.2 us (97%)
  local copies, waits for them, and re-layouts  1.26 us (3%)
    pallas_call x1, Pallas kernels, shards(): pl.pallas_call(functools.partial(kernel, rows, cols), out_shape=jax.Shape...  42.2 us
    unnamed x1, local copies, waits for them, and re-layouts  1.26 us

profile of v1, /device:TPU:0, one launch (start us, length us, event | category | flops | bytes accessed | tf_op | source)
XLA Modules:
  0.0 43.5 jit_solution(714569261409530443)
XLA Ops:
  0.0 42.2 %shard_map.64 = f32[2,2,16]{2,1,0:T(2,128)} custom-call(bf16[1,2,128,512]{3,2,1,0:T(8,128)(2,1)} %src_ref.1, bf16[2,2,128,512]{3,2,1,0:T(8,128)(2,1)} %snk_ref.1, bf16[1,2,2,512,512]{4,3,2,1,0:T(8,128)(2,1)} %per_ref.1, s32[2,16]{1,0:T(2,128)} %ins_ref.1, f32[16,4096]{1,0:T(8,128)} %constant.4.clone.second_ref, f32[16,4096]{1,0:T(8,128)} %constant.5.clone.first_ref), custom_call_target="tpu_custom_call" | custom-call | tf_op jit(solution)/shard_map/pallas_call | solution.py:363
  42.2 1.3 %copy.8 = f32[2,16,1,2]{1,3,2,0:T(2,128)} copy(f32[2,16,1,2]{1,3,2,0:T(2,128)} %bitcast.3) | data formatting | bytes 512

commit v2 on v1

--- a/solution.py
+++ b/solution.py
@@ -118,15 +118,15 @@
             device_id_type=MESH,
         )
 
-    for sink in range(sinks):
-
-        @pl.when(row < rows - 1)
-        def _():
-            hop(row, sink, 0, snk_ref.at[sink]).start()
-
-        @pl.when(row > 0)
-        def _():
-            hop(row, sink, 1, snk_ref.at[sink]).start()
+    near = 2 * row // rows
+    for turn in range(2):
+        for sink in range(sinks):
+            for way in range(2):
+                there = row < rows - 1 if way == 0 else row > 0
+
+                @pl.when(jnp.logical_and(there, (near + way + turn) % 2 == 1))
+                def _():
+                    hop(row, sink, way, snk_ref.at[sink]).start()
 
     def spread(step):
         return pltpu.make_async_remote_copy(
@@ -284,17 +284,17 @@
             return carry
 
         lax.fori_loop(0, sinks, own, 0)
-        for step in range(1, rows - 1):
+        for step in range(1, rows - 2):
             for sink in range(sinks):
                 arrive(step, sink)
-                if step < rows - 2:
-                    both_ways(step - 1, sink)
-                else:
-                    if sink == 0:
-                        lax.fori_loop(
-                            0, sinks, lambda k, carry: (both_ways(step - 1, k), carry)[1], 0
-                        )
-                    both_ways(step, sink)
+                both_ways(step - 1, sink)
+        for sink in range(sinks):
+            if rows > 2:
+                both_ways(rows - 3, sink)
+        for sink in range(sinks):
+            if rows > 2:
+                arrive(rows - 2, sink)
+            both_ways(rows - 2, sink)
     else:
         def pass_on(step, carry):
             for sink in range(sinks):

time: 43.6 us -> 43.6 us (level)
  no operation moved by 1% of the time
where the time goes in v2:
time: 43.6 us; the launch traced here: 43.4 us
  Pallas kernels  42.2 us (97%)
  local copies, waits for them, and re-layouts  1.26 us (3%)
    pallas_call x1, Pallas kernels, shards(): pl.pallas_call(functools.partial(kernel, rows, cols), out_shape=jax.Shape...  42.2 us
    unnamed x1, local copies, waits for them, and re-layouts  1.26 us

profile of v2, /device:TPU:0, one launch (start us, length us, event | category | flops | bytes accessed | tf_op | source)
XLA Modules:
  0.0 43.4 jit_solution(18444794903113495250)
XLA Ops:
  0.0 42.2 %shard_map.64 = f32[2,2,16]{2,1,0:T(2,128)} custom-call(bf16[1,2,128,512]{3,2,1,0:T(8,128)(2,1)} %src_ref.1, bf16[2,2,128,512]{3,2,1,0:T(8,128)(2,1)} %snk_ref.1, bf16[1,2,2,512,512]{4,3,2,1,0:T(8,128)(2,1)} %per_ref.1, s32[2,16]{1,0:T(2,128)} %ins_ref.1, f32[16,4096]{1,0:T(8,128)} %constant.4.clone.second_ref, f32[16,4096]{1,0:T(8,128)} %constant.5.clone.first_ref), custom_call_target="tpu_custom_call" | custom-call | tf_op jit(solution)/shard_map/pallas_call | solution.py:363
  42.2 1.3 %copy.8 = f32[2,16,1,2]{1,3,2,0:T(2,128)} copy(f32[2,16,1,2]{1,3,2,0:T(2,128)} %bitcast.3) | data formatting | bytes 512

commit v3 on v2

--- a/solution.py
+++ b/solution.py
@@ -236,10 +236,9 @@
                         rhs[s, c, h, :, g * evecs : (g + 1) * evecs] = piece[start : start + SUB]
         right = rhs[...].reshape(width, groups * evecs)
         sums = []
-        for u in range(4):
-            left = lhs[sink, u].reshape(width, groups * evecs)
-            full = dot_trans(left, right).reshape(16, SUB, width)
-            sums.append(jnp.sum(full * mask[None], axis=1))
+        left = lhs[sink].reshape(4 * width, groups * evecs)
+        full = dot_trans(left, right).reshape(64, SUB, width)
+        sums.append(jnp.sum(full * mask[None], axis=1))
         place = jnp.where(to // 8 == sink, signed, 0.0).astype(jnp.bfloat16)
         pair = jnp.concatenate(split(jnp.concatenate(sums, axis=0)), axis=1)
         spins[w] += jnp.dot(

time: 43.6 us -> 43.7 us (level)
  no operation moved by 1% of the time
where the time goes in v3:
time: 43.7 us; the launch traced here: 43.5 us
  Pallas kernels  42.2 us (97%)
  local copies, waits for them, and re-layouts  1.26 us (3%)
    pallas_call x1, Pallas kernels, shards(): pl.pallas_call(functools.partial(kernel, rows, cols), out_shape=jax.Shape...  42.2 us
    unnamed x1, local copies, waits for them, and re-layouts  1.26 us

profile of v3, /device:TPU:0, one launch (start us, length us, event | category | flops | bytes accessed | tf_op | source)
XLA Modules:
  0.0 43.5 jit_solution(16803626068812389553)
XLA Ops:
  0.0 42.2 %shard_map.64 = f32[2,2,16]{2,1,0:T(2,128)} custom-call(bf16[1,2,128,512]{3,2,1,0:T(8,128)(2,1)} %src_ref.1, bf16[2,2,128,512]{3,2,1,0:T(8,128)(2,1)} %snk_ref.1, bf16[1,2,2,512,512]{4,3,2,1,0:T(8,128)(2,1)} %per_ref.1, s32[2,16]{1,0:T(2,128)} %ins_ref.1, f32[16,4096]{1,0:T(8,128)} %constant.4.clone.second_ref, f32[16,4096]{1,0:T(8,128)} %constant.5.clone.first_ref), custom_call_target="tpu_custom_call" | custom-call | tf_op jit(solution)/shard_map/pallas_call | solution.py:362
  42.2 1.3 %copy.8 = f32[2,16,1,2]{1,3,2,0:T(2,128)} copy(f32[2,16,1,2]{1,3,2,0:T(2,128)} %bitcast.3) | data formatting | bytes 512
